TPU v7x, 32 devices: a whole 2x2x4 slice. The times are simulated.
32 devices in a mesh: outer: 8 (over z, core), inner: 4 (over y, x).
Axes of the slice: x: 2, y: 2, z: 4, core: 2. Of those that a mesh axis runs over, the one named last changes fastest.
Arguments:
- queries: bfloat16 [4096, 32, 128], P(('outer', 'inner')), may hold values from -8 to 8
- keys: bfloat16 [4096, 4, 128], P(('outer', 'inner')), may hold values from -8 to 8
- values: bfloat16 [4096, 4, 128], P(('outer', 'inner')), may hold values from -6 to 6
- positions: int32 [4096], P(('outer', 'inner')), may hold values from 0 to 4095, as said below
Outputs:
- attended: bfloat16 [4096, 32, 128], P(('outer', 'inner'))
Inputs may be any that keep to these rules, and one draw needn't show every extreme that they name: positions is a permutation of the numbers 0 to 4095 made of runs of 64 consecutive ascending positions starting at multiples of 64; runs are laid out in an order drawn from the seed.
All inputs are finite; a program needn't handle non-finite values.
Results may differ from a plain program's by a relative error of at most 0.0045.
Values may be sent and summed in bfloat16 or wider, within the bound.
No kernel may reach another device: no remote copies, remote signals or barrier semaphores. Data moves between devices by JAX's collectives and lax.ppermute only.
A program may use at most 128 MiB of HBM per device.

v0:
```python
import functools
import math

import jax
import jax.numpy as jnp
from jax import lax
from jax.experimental import pallas as pl
from jax.experimental.pallas import tpu as pltpu
from jax.sharding import PartitionSpec as P

RUN = 64
TILE = 4
AXES = ("outer", "inner")


def scores(qt, k):
    score = jnp.dot(k, qt, preferred_element_type=jnp.float32)
    return score.reshape(-1, 8, score.shape[1])


def flash(score, vt, state, factor):
    top, total, mixed = state
    new = jnp.max(jnp.max(score, axis=0), axis=0, keepdims=True)
    new = jnp.broadcast_to(new, score.shape[1:])
    if top is not None:
        new = jnp.maximum(top, new)
    weight = jnp.exp2((score - new[None]) * factor)
    part_total = jnp.sum(weight, axis=0)
    weight = weight.reshape(-1, weight.shape[2]).astype(jnp.bfloat16)
    part_mixed = jnp.dot(vt, weight, preferred_element_type=jnp.float32)
    if top is None:
        return new, part_total, part_mixed
    decay = jnp.exp2((top - new) * factor)
    mixed = mixed.reshape(-1, 8, mixed.shape[1]) * decay[None]
    return new, total * decay + part_total, mixed.reshape(part_mixed.shape) + part_mixed


def head_tile(qt_ref, state_refs, a, keys, values, factor, mask=None):
    ahead = scores(qt_ref[a, 0], keys(0))
    heads_kv = qt_ref.shape[1]
    for h in range(heads_kv):
        score = ahead
        if h + 1 < heads_kv:
            ahead = scores(qt_ref[a, h + 1], keys(h + 1))
        if mask is None:
            state = tuple(ref[a, h] for ref in state_refs)
        else:
            score = jnp.where(mask.reshape(score.shape), score, -jnp.inf)
            state = (None, None, None)
        state = flash(score, values(h), state, factor)
        for ref, value in zip(state_refs, state):
            ref[a, h] = value


def own_kernel(group, factor, half, q_ref, own_ref, meta_ref, qt_ref, *refs):
    heads_kv, head_dim, rows = qt_ref.shape[1:]
    state_refs = refs[:3]
    key_rows = heads_kv * RUN
    value_rows = heads_kv * head_dim

    ids = own_ref[2 * key_rows + value_rows :].astype(jnp.float32)
    lane = lax.broadcasted_iota(jnp.int32, ids.shape, 1)
    numbers = [jnp.max(jnp.where(lane // RUN == a, ids, 0.0)) for a in range(2)]
    row = lax.broadcasted_iota(jnp.int32, meta_ref.shape, 0)
    meta_ref[...] = jnp.where(
        row == 0, numbers[0], jnp.where(row == 1, numbers[1], 0.0)
    )

    key_at = lax.broadcasted_iota(jnp.int32, (2 * RUN, rows), 0)
    row_at = lax.broadcasted_iota(jnp.int32, (2 * RUN, rows), 1) // group
    for a in range(2):
        for h in range(heads_kv):
            qt_ref[a, h] = q_ref[a, h].T
        mine, other = numbers[a], numbers[1 - a]
        seen = (other < mine) & ((other >= half) == (mine >= half))
        reach = jnp.where(seen, RUN, 0)
        if a == 0:
            live = (key_at <= row_at) | ((key_at >= RUN) & (key_at < RUN + reach))
        else:
            live = (key_at < reach) | ((key_at >= RUN) & (key_at - RUN <= row_at))

        def keys(h):
            parts = [own_ref[n : n + RUN] for n in (h * RUN, key_rows + h * RUN)]
            return jnp.concatenate(parts)

        def values(h):
            start = 2 * key_rows + h * head_dim
            return own_ref[start : start + head_dim]

        head_tile(qt_ref, state_refs, a, keys, values, factor, live)


def attend_kernel(group, factor, half, last, blocks, qt_ref, *refs):
    heads_kv, head_dim, rows = qt_ref.shape[1:]
    key_rows = heads_kv * RUN
    value_rows = heads_kv * head_dim
    block_rows = 2 * key_rows + value_rows + 16
    kv_refs, refs = refs[: len(blocks)], refs[len(blocks) :]
    refs = refs[6:]
    if last:
        out_ref, refs = refs[0], refs[1:]
    meta_ref, *state_refs, kbuf, vbuf = refs

    meta = meta_ref[...]
    counts = tuple(
        jnp.max(meta[2 + a : 3 + a]).astype(jnp.int32) for a in range(2)
    )
    seen_bits = []
    for ref, (skip, end) in zip(kv_refs, blocks):
        assert end - skip <= 8
        ids = jnp.concatenate(
            [ref[n * block_rows - 16 : n * block_rows] for n in range(skip + 1, end + 1)]
        ).astype(jnp.float32)
        row = lax.broadcasted_iota(jnp.int32, ids.shape, 0)
        lane = lax.broadcasted_iota(jnp.int32, ids.shape, 1)
        bit = jnp.left_shift(1, 2 * (row // 16) + lane // RUN)
        bit = jnp.where((row % 16 == 0) & (lane % RUN == 0), bit, 0).astype(jnp.float32)
        found = []
        for a in range(2):
            mine = meta[a : a + 1]
            low = jnp.where(mine >= half, float(half), 0.0)
            seen = (ids < mine) & (ids >= low)
            found.append(jnp.sum(jnp.where(seen, bit, 0.0)).astype(jnp.int32))
        seen_bits.append(found)

    lane = lax.broadcasted_iota(jnp.int32, (value_rows, 2 * RUN), 1)
    for ref, (skip, end), bits in zip(kv_refs, blocks, seen_bits):

        def gather(n, counts):
            start = (skip + n // 2) * block_rows
            side = n % 2
            fresh = []
            for a in range(2):
                flag = (bits[a] >> n) & 1
                count = counts[a]

                @pl.when(flag == 1)
                def _():
                    at = pl.multiple_of(start + side * key_rows, 16)
                    kbuf[a, count] = ref[pl.ds(at, key_rows), :]
                    at = pl.multiple_of(start + 2 * key_rows, 16)
                    value = ref[pl.ds(at, value_rows), :]
                    parity = count % 2
                    pair = count // 2
                    value = jnp.where(
                        parity == side, value, pltpu.roll(value, RUN, 1)
                    )
                    vbuf[a, pair] = jnp.where(
                        lane // RUN == parity, value, vbuf[a, pair]
                    )

                fresh.append(count + flag)
            return tuple(fresh)

        counts = lax.fori_loop(0, 2 * (end - skip), gather, counts)

    def some_runs(a, start, runs):
        def keys(h):
            found = kbuf[a, pl.ds(start, runs), h * RUN : (h + 1) * RUN, :]
            return found.reshape(runs * RUN, -1)

        def values(h):
            found = [
                vbuf[a, start // 2 + n, h * head_dim : (h + 1) * head_dim, :]
                for n in range((runs + 1) // 2)
            ]
            return jnp.concatenate(found, axis=1)[:, : runs * RUN]

        head_tile(qt_ref, state_refs, a, keys, values, factor)

    whole = [count // TILE for count in counts]

    def step(item, carry):
        a = (item >= whole[0]).astype(jnp.int32)
        some_runs(a, (item - a * whole[0]) * TILE, TILE)
        return carry

    lax.fori_loop(0, whole[0] + whole[1], step, 0)

    if not last:
        row = lax.broadcasted_iota(jnp.int32, meta.shape, 0)
        for a in range(2):
            start = whole[a] * TILE
            rest = counts[a] - start

            @pl.when((whole[a] > 0) & (rest > 0))
            def _():
                for n in range(TILE - 1):
                    kbuf[a, n] = kbuf[a, start + n]
                for n in range(TILE // 2):
                    vbuf[a, n] = vbuf[a, start // 2 + n]

            meta = jnp.where(row == 2 + a, rest.astype(jnp.float32), meta)
        meta_ref[...] = meta
        return

    for a in range(2):
        start = whole[a] * TILE
        rest = counts[a] - start
        runs = TILE // 2
        while runs:

            @pl.when(rest & runs != 0)
            def _():
                some_runs(a, start, runs)

            start = start + (rest & runs)
            runs //= 2
        for h in range(0, heads_kv, 2):
            done = []
            for g in (h, h + 1):
                total = jnp.sum(state_refs[1][a, g], axis=0, keepdims=True)
                part = state_refs[2][a, g] * (1.0 / total)
                done.append(part.T.reshape(RUN, group, -1))
            out_ref[a * RUN : (a + 1) * RUN, h * group : (h + 2) * group, :] = (
                jnp.concatenate(done, axis=1).astype(out_ref.dtype)
            )


class Attention:
    def __init__(self, q, group, half, room):
        self.q, self.group, self.half = q, group, half
        self.factor = math.log2(math.e) / math.sqrt(q.shape[3])
        heads_kv, rows, head_dim = q.shape[1:]
        self.block_rows = 2 * heads_kv * RUN + heads_kv * head_dim + 16
        slots = 2 * room + TILE
        self.carried = [jax.ShapeDtypeStruct((8, 128), jnp.float32)]
        self.carried += [
            jax.ShapeDtypeStruct((2, heads_kv, n, rows), jnp.float32)
            for n in (8, 8, head_dim)
        ]
        self.carried += [
            jax.ShapeDtypeStruct((2, slots, heads_kv * RUN, head_dim), q.dtype),
            jax.ShapeDtypeStruct((2, slots // 2, heads_kv * head_dim, 2 * RUN), q.dtype),
        ]

    def call(self, kernel, operands, shapes, aliases, count, name):
        vmem = pl.BlockSpec(memory_space=pltpu.VMEM)
        return pl.pallas_call(
            kernel,
            out_shape=shapes,
            in_specs=[vmem] * len(operands),
            out_specs=[vmem] * len(shapes),
            input_output_aliases=aliases,
            compiler_params=pltpu.CompilerParams(vmem_limit_bytes=24 * 1024 * 1024),
            cost_estimate=pl.CostEstimate(
                flops=count * RUN * self.q.size * 4,
                bytes_accessed=self.q.size * 8,
                transcendentals=0,
            ),
            name=name,
        )(*operands)

    def start(self, own):
        kernel = functools.partial(own_kernel, self.group, self.factor, self.half)
        heads_kv, rows, head_dim = self.q.shape[1:]
        qt = jax.ShapeDtypeStruct((2, heads_kv, head_dim, rows), self.q.dtype)
        shapes = [self.carried[0], qt] + self.carried[1:]
        meta, self.qt, *rest = self.call(
            kernel, [self.q, own], shapes, {}, 2, "attend_own"
        )
        return [meta, *rest]

    def add(self, state, kvs, out=None):
        kvs = [x if isinstance(x, tuple) else (x, 0) for x in kvs]
        blocks = [(skip, x.shape[0] // self.block_rows) for x, skip in kvs]
        count = sum(end - skip for skip, end in blocks)
        operands = [self.qt, *(x for x, _ in kvs), *state]
        first, ahead = 1 + len(kvs), int(out is not None)
        aliases = {first + n: ahead + n for n in range(len(state))}
        shapes = ([out] if ahead else []) + self.carried
        kernel = functools.partial(
            attend_kernel, self.group, self.factor, self.half, out is not None, blocks
        )
        results = self.call(kernel, operands, shapes, aliases, count, "attend")
        return results[0] if ahead else results


def per_device(queries, keys, values, positions):
    outer, inner = lax.axis_size("outer"), lax.axis_size("inner")
    tokens, heads_q, head_dim = queries.shape
    heads_kv = keys.shape[1]
    group = heads_q // heads_kv
    half = tokens // RUN * outer * inner // 2

    chips = outer // 2
    bits = inner.bit_length() - 1
    ring = [0] + list(range(1, chips, 2)) + list(range(2, chips, 2))[::-1]
    after = {ring[n]: ring[(n + 1) % chips] for n in range(chips)}

    def permute(x, to):
        pairs = []
        for z in range(chips):
            for core in range(2):
                for place in range(inner):
                    nz, ncore, nplace = to(z, core, place)
                    pairs.append(
                        (
                            (2 * z + core) * inner + place,
                            (2 * nz + ncore) * inner + nplace,
                        )
                    )
        return lax.ppermute(x, AXES, pairs)

    def along_z(x):
        return permute(x, lambda z, core, place: (after[z], core, place))

    def over_place(x, step):
        def to(z, core, place):
            return z, core, place ^ (1 << (bits - 1 - step if core else step))

        return permute(x, to)

    def other_core(x):
        return permute(x, lambda z, core, place: (z, 1 - core, place))

    def tied(x, *others):
        return lax.optimization_barrier((x, *others))[0]

    by_run = keys.reshape(2, RUN, heads_kv, head_dim).transpose(0, 2, 1, 3)
    numbers = (positions // RUN).astype(jnp.bfloat16)
    own = jnp.concatenate(
        [
            by_run.reshape(-1, head_dim),
            values.reshape(tokens, -1).T,
            jnp.broadcast_to(numbers[None, :], (16, tokens)),
        ]
    )
    q = (
        queries.reshape(2, RUN, heads_kv, group, head_dim)
        .transpose(0, 2, 1, 3, 4)
        .reshape(2, heads_kv, RUN * group, head_dim)
    )

    attention = Attention(q, group, half, 2 * inner)
    state = attention.start(own)
    planes, done = [own], []
    near, far = [], []

    for n in range(chips):
        stage = planes[n]
        if n + 1 < chips:
            planes.append(along_z(stage))
        if n > 0:
            stage = tied(stage, *near[n - 1][1:], *(far[n - 2] if n > 1 else []))
        near.append([stage] + [over_place(stage, step) for step in range(bits)])
        late = near[n][1]
        if n + 1 < chips:
            late = tied(late, planes[n + 1])
        if n > 1:
            state = attention.add(state, done[n - 2])
        late = tied(late, state[0])
        reached = {0: stage}
        for step in range(bits):
            reached[1 << step] = near[n][1 + step]
        far.append([])
        for step in range(1, bits):
            for place in range(1, 1 << step):
                source = late if place == 1 else reached[place]
                reached[place | (1 << step)] = over_place(source, step)
                far[n].append(reached[place | (1 << step)])
        if n + 1 < chips:
            mine = jnp.concatenate(near[n] + far[n])
            done.append([(mine, int(n == 0)), other_core(mine)])
    most = jnp.concatenate(near[-1] + far[-1][:-1])
    theirs = other_core(most)
    state = attention.add(state, done[-1])
    state = attention.add(state, [most])
    final = tied(far[-1][-1], state[0])
    final_theirs = other_core(final)
    state = attention.add(state, [theirs, final])
    out = jax.ShapeDtypeStruct(queries.shape, queries.dtype)
    return attention.add(state, [final_theirs], out)


def solution(mesh):
    in_specs = (
        P(("outer", "inner"), None, None),
        P(("outer", "inner"), None, None),
        P(("outer", "inner"), None, None),
        P(("outer", "inner")),
    )
    out_specs = P(("outer", "inner"), None, None)
    return jax.shard_map(
        per_device, mesh=mesh, in_specs=in_specs, out_specs=out_specs, check_vma=False
    )
```

profile of v0, /device:TPU:12, one launch (start us, length us, event | category | flops | bytes accessed | tf_op | source)
XLA Modules:
  0.0 72.6 jit_solution(1976306482338291062)
XLA Ops:
  0.0 0.8 %fusion = bf16[128]{0:T(256)(128)(2,1)S(1)} fusion(s32[128]{0:T(128)} %param.7), kind=kLoop, calls=%fused_computation.23 | loop fusion | flops 2048 | bytes 768 | tf_op jit(solution)/shard_map/convert_element_type | solution.py:321
  0.8 1.0 %copy.43 = bf16[128,4,128]{0,2,1:T(8,128)(2,1)S(1)} copy(bf16[128,4,128]{2,1,0:T(4,128)(2,1)} %param.6) | data formatting | bytes 262144 | tf_op args[2]
  1.8 0.9 %copy.42 = bf16[2,64,4,128]{3,1,2,0:T(8,128)(2,1)S(1)} copy(bf16[2,64,4,128]{3,2,1,0:T(4,128)(2,1)} %bitcast.19) | data formatting | bytes 262144 | tf_op jit(solution)/shard_map/reshape | solution.py:320
  2.8 2.6 %collective-permute-start = (bf16[1040,128]{1,0:T(8,128)(2,1)S(1)}, bf16[1040,128]{1,0:T(8,128)(2,1)S(1)}, u32[]{:S(2)}, u32[]{:S(2)}) collective-permute-start(bf16[1040,128]{1,0:T(8,128)(2,1)S(1)} %pad_maximum_fusion.own_ref), channel_id=1, source_target_pairs={{0,8},{1,9},{2,10},{3,11},{4,12},{5,13},{6,14},{7,15},{8,24},{9,25... | collective-permute-start | bytes 798728 | tf_op jit(solution)/shard_map/ppermute | solution.py:303
  5.4 1.5 %collective-permute-start.3 = (bf16[1040,128]{1,0:T(8,128)(2,1)S(1)}, bf16[1040,128]{1,0:T(8,128)(2,1)S(1)}, u32[]{:S(2)}, u32[]{:S(2)}) collective-permute-start(bf16[1040,128]{1,0:T(8,128)(2,1)S(1)} %pad_maximum_fusion.own_ref), channel_id=1, source_target_pairs={{0,1},{1,0},{2,3},{3,2},{4,6},{5,7},{6,4},{7,5},{8,9},{9,8},{10,11... | collective-permute-start | bytes 798728 | tf_op jit(solution)/shard_map/ppermute | solution.py:303
  6.9 0.5 collective-permute-start.4
  7.5 0.2 copy.45
  7.6 1.3 %attend_own.1 = (f32[8,128]{1,0:T(8,128)S(1)}, bf16[2,4,128,512]{3,2,1,0:T(8,128)(2,1)S(1)}, f32[2,4,8,512]{3,2,1,0:T(8,128)S(1)}, f32[2,4,8,512]{3,2,1,0:T(8,12...) custom-call(bf16[2,4,512,128]{3,2,1,0:T(8,128)(2,1)S(1)} %bitcast.13, ...), custom_call_target="tpu_custom_call" | custom-call | flops 268435456 | bytes 4194304 | tf_op jit(solution)/shard_map/attend_own/pallas_call | solution.py:239
  9.0 2.1 %collective-permute-done = bf16[1040,128]{1,0:T(8,128)(2,1)S(1)} collective-permute-done((bf16[1040,128]{1,0:T(8,128)(2,1)S(1)}, bf16[1040,128]{1,0:T(8,128)(2,1)S(1)}, u32[]{:S(2)}, u32[]{:S(2)}) %collective-permute-start) | collective-permute-done | bytes 266272 | tf_op jit(solution)/shard_map/ppermute | solution.py:303
  11.1 2.4 %collective-permute-done.3 = bf16[1040,128]{1,0:T(8,128)(2,1)S(1)} collective-permute-done((bf16[1040,128]{1,0:T(8,128)(2,1)S(1)}, bf16[1040,128]{1,0:T(8,128)(2,1)S(1)}, u32[]{:S(2)}, u32[]{:S(2)}) %collective-permute-start.3) | collective-permute-done | bytes 266272 | tf_op jit(solution)/shard_map/ppermute | solution.py:303
  13.5 0.0 collective-permute-done.4
  13.5 1.5 %collective-permute-start.5 = (bf16[1040,128]{1,0:T(8,128)(2,1)S(1)}, bf16[1040,128]{1,0:T(8,128)(2,1)S(1)}, u32[]{:S(2)}, u32[]{:S(2)}) collective-permute-start(bf16[1040,128]{1,0:T(8,128)(2,1)S(1)} %collective-permute-done), channel_id=1, source_target_pairs={{0,1},{1,0},{2,3},{3,2},{4,6},{5,7},{6,4},{7,5},{8,9},{9,8},{10,11... | collective-permute-start | bytes 798728 | tf_op jit(solution)/shard_map/ppermute | solution.py:303
  15.0 1.5 %collective-permute-start.6 = (bf16[1040,128]{1,0:T(8,128)(2,1)S(1)}, bf16[1040,128]{1,0:T(8,128)(2,1)S(1)}, u32[]{:S(2)}, u32[]{:S(2)}) collective-permute-start(bf16[1040,128]{1,0:T(8,128)(2,1)S(1)} %collective-permute-done), channel_id=1, source_target_pairs={{0,2},{1,3},{2,0},{3,1},{4,5},{5,4},{6,7},{7,6},{8,10},{9,11},{10,... | collective-permute-start | bytes 798728 | tf_op jit(solution)/shard_map/ppermute | solution.py:303
  16.5 0.5 collective-permute-start.7
  17.0 1.0 %collective-permute-start.1 = (bf16[1040,128]{1,0:T(8,128)(2,1)S(1)}, bf16[1040,128]{1,0:T(8,128)(2,1)S(1)}, u32[]{:S(2)}, u32[]{:S(2)}) collective-permute-start(bf16[1040,128]{1,0:T(8,128)(2,1)S(1)} %collective-permute-done), channel_id=1, source_target_pairs={{0,8},{1,9},{2,10},{3,11},{4,12},{5,13},{6,14},{7,15},{8,24},{9,25... | collective-permute-start | bytes 798728 | tf_op jit(solution)/shard_map/ppermute | solution.py:303
  18.0 6.3 %collective-permute-done.7 = bf16[1040,128]{1,0:T(8,128)(2,1)S(1)} collective-permute-done((bf16[1040,128]{1,0:T(8,128)(2,1)S(1)}, bf16[1040,128]{1,0:T(8,128)(2,1)S(1)}, u32[]{:S(2)}, u32[]{:S(2)}) %collective-permute-start.7) | collective-permute-done | bytes 266272 | tf_op jit(solution)/shard_map/ppermute | solution.py:303
  24.4 1.1 %collective-permute-start.13 = (bf16[4160,128]{1,0:T(8,128)(2,1)S(1)}, bf16[4160,128]{1,0:T(8,128)(2,1)S(1)}, u32[]{:S(2)}, u32[]{:S(2)}) collective-permute-start(bf16[4160,128]{1,0:T(8,128)(2,1)S(1)} %constant_dynamic-update-slice_fusion.4.refs_0_), channel_id=1, source_target_pairs={{0,4},{1,5},{2,6},{3,7},{4,0},{5,1},{6,2},{7,3},{8,12},{9,13},{10,... | collective-permute-start | bytes 3194888 | tf_op jit(solution)/shard_map/ppermute | solution.py:303
  25.6 0.0 collective-permute-done.5
  25.6 0.0 collective-permute-done.1
  25.6 0.0 collective-permute-done.6
  25.6 1.6 %collective-permute-start.8 = (bf16[1040,128]{1,0:T(8,128)(2,1)S(1)}, bf16[1040,128]{1,0:T(8,128)(2,1)S(1)}, u32[]{:S(2)}, u32[]{:S(2)}) collective-permute-start(bf16[1040,128]{1,0:T(8,128)(2,1)S(1)} %collective-permute-done.1), channel_id=1, source_target_pairs={{0,1},{1,0},{2,3},{3,2},{4,6},{5,7},{6,4},{7,5},{8,9},{9,8},{10,11... | collective-permute-start | bytes 798728 | tf_op jit(solution)/shard_map/ppermute | solution.py:303
  27.1 0.8 %collective-permute-start.9 = (bf16[1040,128]{1,0:T(8,128)(2,1)S(1)}, bf16[1040,128]{1,0:T(8,128)(2,1)S(1)}, u32[]{:S(2)}, u32[]{:S(2)}) collective-permute-start(bf16[1040,128]{1,0:T(8,128)(2,1)S(1)} %collective-permute-done.1), channel_id=1, source_target_pairs={{0,2},{1,3},{2,0},{3,1},{4,5},{5,4},{6,7},{7,6},{8,10},{9,11},{10,... | collective-permute-start | bytes 798728 | tf_op jit(solution)/shard_map/ppermute | solution.py:303
  27.9 1.2 %collective-permute-start.10 = (bf16[1040,128]{1,0:T(8,128)(2,1)S(1)}, bf16[1040,128]{1,0:T(8,128)(2,1)S(1)}, u32[]{:S(2)}, u32[]{:S(2)}) collective-permute-start(bf16[1040,128]{1,0:T(8,128)(2,1)S(1)} %collective-permute-done.5), channel_id=1, source_target_pairs={{0,2},{1,3},{2,0},{3,1},{4,5},{5,4},{6,7},{7,6},{8,10},{9,11},{10,... | collective-permute-start | bytes 798728 | tf_op jit(solution)/shard_map/ppermute | solution.py:303
  29.2 0.7 collective-permute-start.2
  29.9 5.0 %collective-permute-done.8 = bf16[1040,128]{1,0:T(8,128)(2,1)S(1)} collective-permute-done((bf16[1040,128]{1,0:T(8,128)(2,1)S(1)}, bf16[1040,128]{1,0:T(8,128)(2,1)S(1)}, u32[]{:S(2)}, u32[]{:S(2)}) %collective-permute-start.8) | collective-permute-done | bytes 266272 | tf_op jit(solution)/shard_map/ppermute | solution.py:303
  34.9 1.4 %collective-permute-done.2 = bf16[1040,128]{1,0:T(8,128)(2,1)S(1)} collective-permute-done((bf16[1040,128]{1,0:T(8,128)(2,1)S(1)}, bf16[1040,128]{1,0:T(8,128)(2,1)S(1)}, u32[]{:S(2)}, u32[]{:S(2)}) %collective-permute-start.2) | collective-permute-done | bytes 266272 | tf_op jit(solution)/shard_map/ppermute | solution.py:303
  36.3 0.0 collective-permute-done.9
  36.3 0.5 collective-permute-done.10
  36.8 1.5 %collective-permute-start.11 = (bf16[1040,128]{1,0:T(8,128)(2,1)S(1)}, bf16[1040,128]{1,0:T(8,128)(2,1)S(1)}, u32[]{:S(2)}, u32[]{:S(2)}) collective-permute-start(bf16[1040,128]{1,0:T(8,128)(2,1)S(1)} %collective-permute-done.2), channel_id=1, source_target_pairs={{0,1},{1,0},{2,3},{3,2},{4,6},{5,7},{6,4},{7,5},{8,9},{9,8},{10,11... | collective-permute-start | bytes 798728 | tf_op jit(solution)/shard_map/ppermute | solution.py:303
  38.3 1.2 %collective-permute-start.15 = (bf16[1040,128]{1,0:T(8,128)(2,1)S(1)}, bf16[1040,128]{1,0:T(8,128)(2,1)S(1)}, u32[]{:S(2)}, u32[]{:S(2)}) collective-permute-start(bf16[1040,128]{1,0:T(8,128)(2,1)S(1)} %collective-permute-done.2), channel_id=1, source_target_pairs={{0,2},{1,3},{2,0},{3,1},{4,5},{5,4},{6,7},{7,6},{8,10},{9,11},{10,... | collective-permute-start | bytes 798728 | tf_op jit(solution)/shard_map/ppermute | solution.py:303
  39.5 0.1 collective-permute-start.12
  39.6 2.3 %attend.6 = (f32[8,128]{1,0:T(8,128)S(1)}, f32[2,4,8,512]{3,2,1,0:T(8,128)S(1)}, f32[2,4,8,512]{3,2,1,0:T(8,128)S(1)}, f32[2,4,128,512]{3,2,1,0:T(8,128)S(1)}, b...) custom-call(bf16[2,4,128,512]{3,2,1,0:T(8,128)(2,1)S(1)} %get-tuple-, ...), custom_call_target="tpu_custom_call", output_to_operand_aliasing={{0}: (3, {}), {1}: (4, {}), {2}: (5, {}), {3}: (6, {}), {4}... | custom-call | flops 939524096 | bytes 4194304 | tf_op jit(solution)/shard_map/attend/pallas_call | solution.py:239
  41.9 0.1 collective-permute-start.16
  42.0 6.6 %collective-permute-done.16 = bf16[1040,128]{1,0:T(8,128)(2,1)S(1)} collective-permute-done((bf16[1040,128]{1,0:T(8,128)(2,1)S(1)}, bf16[1040,128]{1,0:T(8,128)(2,1)S(1)}, u32[]{:S(2)}, u32[]{:S(2)}) %collective-permute-start.16) | collective-permute-done | bytes 266272 | tf_op jit(solution)/shard_map/ppermute | solution.py:303
  48.7 2.0 %collective-permute-start.17 = (bf16[4160,128]{1,0:T(8,128)(2,1)S(1)}, bf16[4160,128]{1,0:T(8,128)(2,1)S(1)}, u32[]{:S(2)}, u32[]{:S(2)}) collective-permute-start(bf16[4160,128]{1,0:T(8,128)(2,1)S(1)} %constant_dynamic-update-slice_fusion.13.refs_0_), channel_id=1, source_target_pairs={{0,4},{1,5},{2,6},{3,7},{4,0},{5,1},{6,2},{7,3},{8,12},{9,13},{10,... | collective-permute-start | bytes 3194888 | tf_op jit(solution)/shard_map/ppermute | solution.py:303
  50.8 0.0 collective-permute-done.15
  50.9 0.1 collective-permute-start.19
  51.0 0.0 collective-permute-done.12.refs_1_
  51.0 3.4 %attend.7 = (f32[8,128]{1,0:T(8,128)S(1)}, f32[2,4,8,512]{3,2,1,0:T(8,128)S(1)}, f32[2,4,8,512]{3,2,1,0:T(8,128)S(1)}, f32[2,4,128,512]{3,2,1,0:T(8,128)S(1)}, b...) custom-call(bf16[2,4,128,512]{3,2,1,0:T(8,128)(2,1)S(1)} %get-tuple-, ...), custom_call_target="tpu_custom_call", output_to_operand_aliasing={{0}: (3, {}), {1}: (4, {}), {2}: (5, {}), {3}: (6, {}), {4}... | custom-call | flops 1073741824 | bytes 4194304 | tf_op jit(solution)/shard_map/attend/pallas_call | solution.py:239
  54.3 0.1 collective-permute-start.14
  54.4 0.9 %attend.8 = (f32[8,128]{1,0:T(8,128)S(1)}, f32[2,4,8,512]{3,2,1,0:T(8,128)S(1)}, f32[2,4,8,512]{3,2,1,0:T(8,128)S(1)}, f32[2,4,128,512]{3,2,1,0:T(8,128)S(1)}, b...) custom-call(bf16[2,4,128,512]{3,2,1,0:T(8,128)(2,1)S(1)} %get-tuple-, ...), custom_call_target="tpu_custom_call", output_to_operand_aliasing={{0}: (3, {}), {1}: (4, {}), {2}: (5, {}), {3}: (6, {}), {4}... | custom-call | flops 1073741824 | bytes 4194304 | tf_op jit(solution)/shard_map/attend/pallas_call | solution.py:239
  55.4 1.8 %attend.9 = (f32[8,128]{1,0:T(8,128)S(1)}, f32[2,4,8,512]{3,2,1,0:T(8,128)S(1)}, f32[2,4,8,512]{3,2,1,0:T(8,128)S(1)}, f32[2,4,128,512]{3,2,1,0:T(8,128)S(1)}, b...) custom-call(bf16[2,4,128,512]{3,2,1,0:T(8,128)(2,1)S(1)} %get-tuple-, ...), custom_call_target="tpu_custom_call", output_to_operand_aliasing={{0}: (2, {}), {1}: (3, {}), {2}: (4, {}), {3}: (5, {}), {4}... | custom-call | flops 402653184 | bytes 4194304 | tf_op jit(solution)/shard_map/attend/pallas_call | solution.py:239
  57.1 3.7 %collective-permute-done.14.refs_1_ = bf16[1040,128]{1,0:T(8,128)(2,1)S(1)} collective-permute-done((bf16[1040,128]{1,0:T(8,128)(2,1)S(1)}, bf16[1040,128]{1,0:T(8,128)(2,1)S(1)}, u32[]{:S(2)}, u32[]{:S(2)}) %collective-permute-start.14) | collective-permute-done | bytes 266272 | tf_op jit(solution)/shard_map/ppermute | solution.py:303
  60.8 4.5 %collective-permute-start.18 = (bf16[1040,128]{1,0:T(8,128)(2,1)S(1)}, bf16[1040,128]{1,0:T(8,128)(2,1)S(1)}, u32[]{:S(2)}, u32[]{:S(2)}) collective-permute-start(bf16[1040,128]{1,0:T(8,128)(2,1)S(1)} %collective-permute-done.14.refs_1_), channel_id=1, source_target_pairs={{0,4},{1,5},{2,6},{3,7},{4,0},{5,1},{6,2},{7,3},{8,12},{9,13},{10,... | collective-permute-start | bytes 798728 | tf_op jit(solution)/shard_map/ppermute | solution.py:303
  65.3 0.0 collective-permute-done.19.refs_0_
  65.3 2.1 %attend.10 = (f32[8,128]{1,0:T(8,128)S(1)}, f32[2,4,8,512]{3,2,1,0:T(8,128)S(1)}, f32[2,4,8,512]{3,2,1,0:T(8,128)S(1)}, f32[2,4,128,512]{3,2,1,0:T(8,128)S(1)}, ...) custom-call(bf16[2,4,128,512]{3,2,1,0:T(8,128)(2,1)S(1)} %get-tuple-, ...), custom_call_target="tpu_custom_call", output_to_operand_aliasing={{0}: (3, {}), {1}: (4, {}), {2}: (5, {}), {3}: (6, {}), {4}... | custom-call | flops 536870912 | bytes 4194304 | tf_op jit(solution)/shard_map/attend/pallas_call | solution.py:239
  67.4 0.0 collective-permute-done.18.refs_0_
  67.4 5.2 %attend.11 = (bf16[128,32,128]{2,1,0:T(8,128)(2,1)}, f32[8,128]{1,0:T(8,128)S(1)}, f32[2,4,8,512]{3,2,1,0:T(8,128)S(1)}, f32[2,4,8,512]{3,2,1,0:T(8,128)S(1)}, f...) custom-call(bf16[2,4,128,512]{3,2,1,0:T(8,128)(2,1)S(1)} %get-tuple-, ...), custom_call_target="tpu_custom_call", output_to_operand_aliasing={{1}: (2, {}), {2}: (3, {}), {3}: (4, {}), {4}: (5, {}), {5}... | custom-call | flops 134217728 | bytes 4194304 | tf_op jit(solution)/shard_map/attend/pallas_call | solution.py:239
  (24 shorter events, 0.5 us)
Async XLA Ops:
  0.0 7.4 %copy-start = (bf16[128,32,128]{2,1,0:T(8,128)(2,1)S(1)}, bf16[128,32,128]{2,1,0:T(8,128)(2,1)}, u32[]{:S(2)}) copy-start(bf16[128,32,128]{2,1,0:T(8,128)(2,1)} %param.4) | copy-start | bytes 3145732
  2.8 8.3 %collective-permute-start = (bf16[1040,128]{1,0:T(8,128)(2,1)S(1)}, bf16[1040,128]{1,0:T(8,128)(2,1)S(1)}, u32[]{:S(2)}, u32[]{:S(2)}) collective-permute-start(bf16[1040,128]{1,0:T(8,128)(2,1)S(1)} %pad_maximum_fusion.own_ref), channel_id=1, source_target_pairs={{0,8},{1,9},{2,10},{3,11},{4,12},{5,13},{6,14},{7,15},{8,24},{9,25... | collective-permute-start | bytes 798728 | tf_op jit(solution)/shard_map/ppermute | solution.py:303
  5.4 8.1 %collective-permute-start.3 = (bf16[1040,128]{1,0:T(8,128)(2,1)S(1)}, bf16[1040,128]{1,0:T(8,128)(2,1)S(1)}, u32[]{:S(2)}, u32[]{:S(2)}) collective-permute-start(bf16[1040,128]{1,0:T(8,128)(2,1)S(1)} %pad_maximum_fusion.own_ref), channel_id=1, source_target_pairs={{0,1},{1,0},{2,3},{3,2},{4,6},{5,7},{6,4},{7,5},{8,9},{9,8},{10,11... | collective-permute-start | bytes 798728 | tf_op jit(solution)/shard_map/ppermute | solution.py:303
  6.9 6.6 %collective-permute-start.4 = (bf16[1040,128]{1,0:T(8,128)(2,1)S(1)}, bf16[1040,128]{1,0:T(8,128)(2,1)S(1)}, u32[]{:S(2)}, u32[]{:S(2)}) collective-permute-start(bf16[1040,128]{1,0:T(8,128)(2,1)S(1)} %pad_maximum_fusion.own_ref), channel_id=1, source_target_pairs={{0,2},{1,3},{2,0},{3,1},{4,5},{5,4},{6,7},{7,6},{8,10},{9,11},{10,... | collective-permute-start | bytes 798728 | tf_op jit(solution)/shard_map/ppermute | solution.py:303
  13.5 12.1 %collective-permute-start.5 = (bf16[1040,128]{1,0:T(8,128)(2,1)S(1)}, bf16[1040,128]{1,0:T(8,128)(2,1)S(1)}, u32[]{:S(2)}, u32[]{:S(2)}) collective-permute-start(bf16[1040,128]{1,0:T(8,128)(2,1)S(1)} %collective-permute-done), channel_id=1, source_target_pairs={{0,1},{1,0},{2,3},{3,2},{4,6},{5,7},{6,4},{7,5},{8,9},{9,8},{10,11... | collective-permute-start | bytes 798728 | tf_op jit(solution)/shard_map/ppermute | solution.py:303
  15.0 10.6 %collective-permute-start.6 = (bf16[1040,128]{1,0:T(8,128)(2,1)S(1)}, bf16[1040,128]{1,0:T(8,128)(2,1)S(1)}, u32[]{:S(2)}, u32[]{:S(2)}) collective-permute-start(bf16[1040,128]{1,0:T(8,128)(2,1)S(1)} %collective-permute-done), channel_id=1, source_target_pairs={{0,2},{1,3},{2,0},{3,1},{4,5},{5,4},{6,7},{7,6},{8,10},{9,11},{10,... | collective-permute-start | bytes 798728 | tf_op jit(solution)/shard_map/ppermute | solution.py:303
  16.5 7.9 %collective-permute-start.7 = (bf16[1040,128]{1,0:T(8,128)(2,1)S(1)}, bf16[1040,128]{1,0:T(8,128)(2,1)S(1)}, u32[]{:S(2)}, u32[]{:S(2)}) collective-permute-start(bf16[1040,128]{1,0:T(8,128)(2,1)S(1)} %collective-permute-done.3), channel_id=1, source_target_pairs={{0,2},{1,3},{2,0},{3,1},{4,5},{5,4},{6,7},{7,6},{8,10},{9,11},{10,... | collective-permute-start | bytes 798728 | tf_op jit(solution)/shard_map/ppermute | solution.py:303
  17.0 8.6 %collective-permute-start.1 = (bf16[1040,128]{1,0:T(8,128)(2,1)S(1)}, bf16[1040,128]{1,0:T(8,128)(2,1)S(1)}, u32[]{:S(2)}, u32[]{:S(2)}) collective-permute-start(bf16[1040,128]{1,0:T(8,128)(2,1)S(1)} %collective-permute-done), channel_id=1, source_target_pairs={{0,8},{1,9},{2,10},{3,11},{4,12},{5,13},{6,14},{7,15},{8,24},{9,25... | collective-permute-start | bytes 798728 | tf_op jit(solution)/shard_map/ppermute | solution.py:303
  24.4 15.2 %collective-permute-start.13 = (bf16[4160,128]{1,0:T(8,128)(2,1)S(1)}, bf16[4160,128]{1,0:T(8,128)(2,1)S(1)}, u32[]{:S(2)}, u32[]{:S(2)}) collective-permute-start(bf16[4160,128]{1,0:T(8,128)(2,1)S(1)} %constant_dynamic-update-slice_fusion.4.refs_0_), channel_id=1, source_target_pairs={{0,4},{1,5},{2,6},{3,7},{4,0},{5,1},{6,2},{7,3},{8,12},{9,13},{10,... | collective-permute-start | bytes 3194888 | tf_op jit(solution)/shard_map/ppermute | solution.py:303
  25.6 9.3 %collective-permute-start.8 = (bf16[1040,128]{1,0:T(8,128)(2,1)S(1)}, bf16[1040,128]{1,0:T(8,128)(2,1)S(1)}, u32[]{:S(2)}, u32[]{:S(2)}) collective-permute-start(bf16[1040,128]{1,0:T(8,128)(2,1)S(1)} %collective-permute-done.1), channel_id=1, source_target_pairs={{0,1},{1,0},{2,3},{3,2},{4,6},{5,7},{6,4},{7,5},{8,9},{9,8},{10,11... | collective-permute-start | bytes 798728 | tf_op jit(solution)/shard_map/ppermute | solution.py:303
  27.1 9.2 %collective-permute-start.9 = (bf16[1040,128]{1,0:T(8,128)(2,1)S(1)}, bf16[1040,128]{1,0:T(8,128)(2,1)S(1)}, u32[]{:S(2)}, u32[]{:S(2)}) collective-permute-start(bf16[1040,128]{1,0:T(8,128)(2,1)S(1)} %collective-permute-done.1), channel_id=1, source_target_pairs={{0,2},{1,3},{2,0},{3,1},{4,5},{5,4},{6,7},{7,6},{8,10},{9,11},{10,... | collective-permute-start | bytes 798728 | tf_op jit(solution)/shard_map/ppermute | solution.py:303
  27.9 8.9 %collective-permute-start.10 = (bf16[1040,128]{1,0:T(8,128)(2,1)S(1)}, bf16[1040,128]{1,0:T(8,128)(2,1)S(1)}, u32[]{:S(2)}, u32[]{:S(2)}) collective-permute-start(bf16[1040,128]{1,0:T(8,128)(2,1)S(1)} %collective-permute-done.5), channel_id=1, source_target_pairs={{0,2},{1,3},{2,0},{3,1},{4,5},{5,4},{6,7},{7,6},{8,10},{9,11},{10,... | collective-permute-start | bytes 798728 | tf_op jit(solution)/shard_map/ppermute | solution.py:303
  29.2 7.1 %collective-permute-start.2 = (bf16[1040,128]{1,0:T(8,128)(2,1)S(1)}, bf16[1040,128]{1,0:T(8,128)(2,1)S(1)}, u32[]{:S(2)}, u32[]{:S(2)}) collective-permute-start(bf16[1040,128]{1,0:T(8,128)(2,1)S(1)} %collective-permute-done.1), channel_id=1, source_target_pairs={{0,8},{1,9},{2,10},{3,11},{4,12},{5,13},{6,14},{7,15},{8,24},{9,25... | collective-permute-start | bytes 798728 | tf_op jit(solution)/shard_map/ppermute | solution.py:303
  36.8 13.9 %collective-permute-start.11 = (bf16[1040,128]{1,0:T(8,128)(2,1)S(1)}, bf16[1040,128]{1,0:T(8,128)(2,1)S(1)}, u32[]{:S(2)}, u32[]{:S(2)}) collective-permute-start(bf16[1040,128]{1,0:T(8,128)(2,1)S(1)} %collective-permute-done.2), channel_id=1, source_target_pairs={{0,1},{1,0},{2,3},{3,2},{4,6},{5,7},{6,4},{7,5},{8,9},{9,8},{10,11... | collective-permute-start | bytes 798728 | tf_op jit(solution)/shard_map/ppermute | solution.py:303
  38.3 12.5 %collective-permute-start.15 = (bf16[1040,128]{1,0:T(8,128)(2,1)S(1)}, bf16[1040,128]{1,0:T(8,128)(2,1)S(1)}, u32[]{:S(2)}, u32[]{:S(2)}) collective-permute-start(bf16[1040,128]{1,0:T(8,128)(2,1)S(1)} %collective-permute-done.2), channel_id=1, source_target_pairs={{0,2},{1,3},{2,0},{3,1},{4,5},{5,4},{6,7},{7,6},{8,10},{9,11},{10,... | collective-permute-start | bytes 798728 | tf_op jit(solution)/shard_map/ppermute | solution.py:303
  39.5 11.5 %collective-permute-start.12 = (bf16[4160,128]{1,0:T(8,128)(2,1)S(1)}, bf16[4160,128]{1,0:T(8,128)(2,1)S(1)}, u32[]{:S(2)}, u32[]{:S(2)}) collective-permute-start(bf16[4160,128]{1,0:T(8,128)(2,1)S(1)} %constant_dynamic-update-slice_fusion.refs_0_), channel_id=1, source_target_pairs={{0,4},{1,5},{2,6},{3,7},{4,0},{5,1},{6,2},{7,3},{8,12},{9,13},{10,... | collective-permute-start | bytes 3194888 | tf_op jit(solution)/shard_map/ppermute | solution.py:303
  41.9 6.8 %collective-permute-start.16 = (bf16[1040,128]{1,0:T(8,128)(2,1)S(1)}, bf16[1040,128]{1,0:T(8,128)(2,1)S(1)}, u32[]{:S(2)}, u32[]{:S(2)}) collective-permute-start(bf16[1040,128]{1,0:T(8,128)(2,1)S(1)} %collective-permute-done.8), channel_id=1, source_target_pairs={{0,2},{1,3},{2,0},{3,1},{4,5},{5,4},{6,7},{7,6},{8,10},{9,11},{10,... | collective-permute-start | bytes 798728 | tf_op jit(solution)/shard_map/ppermute | solution.py:303
  48.7 5.7 %collective-permute-start.17 = (bf16[4160,128]{1,0:T(8,128)(2,1)S(1)}, bf16[4160,128]{1,0:T(8,128)(2,1)S(1)}, u32[]{:S(2)}, u32[]{:S(2)}) collective-permute-start(bf16[4160,128]{1,0:T(8,128)(2,1)S(1)} %constant_dynamic-update-slice_fusion.13.refs_0_), channel_id=1, source_target_pairs={{0,4},{1,5},{2,6},{3,7},{4,0},{5,1},{6,2},{7,3},{8,12},{9,13},{10,... | collective-permute-start | bytes 3194888 | tf_op jit(solution)/shard_map/ppermute | solution.py:303
  50.9 14.4 %collective-permute-start.19 = (bf16[3120,128]{1,0:T(8,128)(2,1)S(1)}, bf16[3120,128]{1,0:T(8,128)(2,1)S(1)}, u32[]{:S(2)}, u32[]{:S(2)}) collective-permute-start(bf16[3120,128]{1,0:T(8,128)(2,1)S(1)} %constant_dynamic-update-slice_fusion.10.refs_0_), channel_id=1, source_target_pairs={{0,4},{1,5},{2,6},{3,7},{4,0},{5,1},{6,2},{7,3},{8,12},{9,13},{10,... | collective-permute-start | bytes 2396168 | tf_op jit(solution)/shard_map/ppermute | solution.py:303
  54.3 6.5 %collective-permute-start.14 = (bf16[1040,128]{1,0:T(8,128)(2,1)S(1)}, bf16[1040,128]{1,0:T(8,128)(2,1)S(1)}, u32[]{:S(2)}, u32[]{:S(2)}) collective-permute-start(bf16[1040,128]{1,0:T(8,128)(2,1)S(1)} %collective-permute-done.11), channel_id=1, source_target_pairs={{0,2},{1,3},{2,0},{3,1},{4,5},{5,4},{6,7},{7,6},{8,10},{9,11},{10,... | collective-permute-start | bytes 798728 | tf_op jit(solution)/shard_map/ppermute | solution.py:303
  60.8 6.6 %collective-permute-start.18 = (bf16[1040,128]{1,0:T(8,128)(2,1)S(1)}, bf16[1040,128]{1,0:T(8,128)(2,1)S(1)}, u32[]{:S(2)}, u32[]{:S(2)}) collective-permute-start(bf16[1040,128]{1,0:T(8,128)(2,1)S(1)} %collective-permute-done.14.refs_1_), channel_id=1, source_target_pairs={{0,4},{1,5},{2,6},{3,7},{4,0},{5,1},{6,2},{7,3},{8,12},{9,13},{10,... | collective-permute-start | bytes 798728 | tf_op jit(solution)/shard_map/ppermute | solution.py:303
where the time goes:
time: 72.9 us; the launch traced here: 72.6 us
  waiting for transfers between devices  28 us (38%)
  starting transfers between devices  23.9 us (33%)
  Pallas kernels  16.9 us (23%)
  local copies, waits for them, and re-layouts  2.64 us (4%)
  other arithmetic  0.77 us (1%)
    ppermute x20, waiting for transfers between devices, permute(): return lax.ppermute(x, AXES, pairs)  28 us
    ppermute x20, starting transfers between devices, permute(): return lax.ppermute(x, AXES, pairs)  23.9 us
    pallas_call x7, Pallas kernels, call(): pl.pallas_call(kernel, out_shape=shapes, in_specs=[vmem] * len(operands),...  16.9 us
  transfers between devices with their start and end apart: 20, of which 8 were waited for; matrix products, arithmetic and copies ran while one was open for 1% of the time, Pallas kernels for 16%

commit v1 on v0

v1 whole, which is shorter than its diff:
```python
import functools
import math

import jax
import jax.numpy as jnp
from jax import lax
from jax.experimental import pallas as pl
from jax.experimental.pallas import tpu as pltpu
from jax.sharding import PartitionSpec as P

RUN = 64
TILE = 8
KEEP = 4
AXES = ("outer", "inner")


def flash(score, v, state, factor, live=None):
    top, total, mixed = state
    keys = score.shape[1]
    if isinstance(live, int):
        lane = lax.broadcasted_iota(jnp.int32, score.shape, 1)
        keys, live = live, lane < live
    if live is not None:
        score = jnp.where(live, score, -jnp.inf)
    parts = [score[:, c : c + 128] for c in range(0, score.shape[1], 128)]
    new = jnp.max(functools.reduce(jnp.maximum, parts), axis=1, keepdims=True)
    if top is None:
        new = jnp.broadcast_to(new, parts[0].shape)
    else:
        new = jnp.maximum(top, new)
    weights = [jnp.exp2((part - new) * factor) for part in parts]
    part_total = functools.reduce(jnp.add, weights)
    weights = jnp.concatenate([w.astype(jnp.bfloat16) for w in weights], axis=1)
    part_mixed = jnp.dot(weights[:, :keys], v, preferred_element_type=jnp.float32)
    if top is None:
        return new, part_total, part_mixed
    decay = jnp.exp2((top - new) * factor)
    return new, total * decay + part_total, mixed * decay + part_mixed


def head_tile(q_ref, state_refs, a, keys, values, factor, live=None):
    def scores(h):
        return jnp.dot(q_ref[a, h], keys(h), preferred_element_type=jnp.float32)

    heads_kv = q_ref.shape[1]
    ahead = scores(0)
    for h in range(heads_kv):
        score = ahead
        if h + 1 < heads_kv:
            ahead = scores(h + 1)
        state = (None, None, None)
        if live is None or isinstance(live, int):
            state = tuple(ref[a, h] for ref in state_refs)
        state = flash(score, values(h), state, factor, live)
        for ref, value in zip(state_refs, state):
            ref[a, h] = value


def own_kernel(group, factor, half, q_ref, own_ref, meta_ref, *refs):
    heads_kv, rows, head_dim = q_ref.shape[1:]
    state_refs = refs[:3]
    key_rows = heads_kv * head_dim
    value_rows = heads_kv * RUN

    ids = own_ref[key_rows + 2 * value_rows :].astype(jnp.float32)
    lane = lax.broadcasted_iota(jnp.int32, ids.shape, 1)
    numbers = [jnp.max(jnp.where(lane // RUN == a, ids, 0.0)) for a in range(2)]
    row = lax.broadcasted_iota(jnp.int32, meta_ref.shape, 0)
    meta_ref[...] = jnp.where(
        row == 0, numbers[0], jnp.where(row == 1, numbers[1], 0.0)
    )

    row_at = lax.broadcasted_iota(jnp.int32, (rows, 2 * RUN), 0) // group
    key_at = lax.broadcasted_iota(jnp.int32, (rows, 2 * RUN), 1)
    for a in range(2):
        mine, other = numbers[a], numbers[1 - a]
        seen = (other < mine) & ((other >= half) == (mine >= half))
        reach = jnp.where(seen, RUN, 0)
        if a == 0:
            live = (key_at <= row_at) | ((key_at >= RUN) & (key_at < RUN + reach))
        else:
            live = (key_at < reach) | ((key_at >= RUN) & (key_at - RUN <= row_at))

        def keys(h):
            return own_ref[h * head_dim : (h + 1) * head_dim]

        def values(h):
            starts = [key_rows + h * RUN, key_rows + value_rows + h * RUN]
            return jnp.concatenate([own_ref[n : n + RUN] for n in starts])

        head_tile(q_ref, state_refs, a, keys, values, factor, live)


def attend_kernel(group, factor, half, last, blocks, q_ref, *refs):
    heads_kv, rows, head_dim = q_ref.shape[1:]
    key_rows = heads_kv * head_dim
    value_rows = heads_kv * RUN
    block_rows = key_rows + 2 * value_rows + 16
    kv_refs, refs = refs[: len(blocks)], refs[len(blocks) :]
    refs = refs[6:]
    if last:
        out_ref, refs = refs[0], refs[1:]
    meta_ref, *state_refs, kbuf, vbuf = refs

    meta = meta_ref[...]
    counts = tuple(
        jnp.max(meta[2 + a : 3 + a]).astype(jnp.int32) for a in range(2)
    )
    seen_bits = []
    for ref, (skip, end) in zip(kv_refs, blocks):
        assert end - skip <= 8
        ids = jnp.concatenate(
            [ref[n * block_rows - 16 : n * block_rows] for n in range(skip + 1, end + 1)]
        ).astype(jnp.float32)
        row = lax.broadcasted_iota(jnp.int32, ids.shape, 0)
        lane = lax.broadcasted_iota(jnp.int32, ids.shape, 1)
        bit = jnp.left_shift(1, 2 * (row // 16) + lane // RUN)
        bit = jnp.where((row % 16 == 0) & (lane % RUN == 0), bit, 0).astype(jnp.float32)
        found = []
        for a in range(2):
            mine = meta[a : a + 1]
            low = jnp.where(mine >= half, float(half), 0.0)
            seen = (ids < mine) & (ids >= low)
            found.append(jnp.sum(jnp.where(seen, bit, 0.0)).astype(jnp.int32))
        seen_bits.append(found)

    lane = lax.broadcasted_iota(jnp.int32, (key_rows, 2 * RUN), 1)
    for ref, (skip, end), bits in zip(kv_refs, blocks, seen_bits):

        def gather(n, counts):
            start = (skip + n // 2) * block_rows
            side = n % 2
            fresh = []
            for a in range(2):
                flag = (bits[a] >> n) & 1
                count = counts[a]

                @pl.when(flag == 1)
                def _():
                    at = pl.multiple_of(start + key_rows + side * value_rows, 16)
                    vbuf[a, count] = ref[pl.ds(at, value_rows), :]
                    key = ref[pl.ds(pl.multiple_of(start, 16), key_rows), :]
                    parity = count % 2
                    pair = count // 2
                    key = jnp.where(parity == side, key, pltpu.roll(key, RUN, 1))
                    kbuf[a, pair] = jnp.where(lane // RUN == parity, key, kbuf[a, pair])

                fresh.append(count + flag)
            return tuple(fresh)

        counts = lax.fori_loop(0, 2 * (end - skip), gather, counts)

    def some_runs(a, start, runs):
        def keys(h):
            found = [
                kbuf[a, start // 2 + n, h * head_dim : (h + 1) * head_dim, :]
                for n in range((runs + 1) // 2)
            ]
            return jnp.concatenate(found, axis=1)

        def values(h):
            found = vbuf[a, pl.ds(start, runs), h * RUN : (h + 1) * RUN, :]
            return found.reshape(runs * RUN, -1)

        live = RUN if runs == 1 else None
        head_tile(q_ref, state_refs, a, keys, values, factor, live)

    whole = [count // TILE for count in counts]

    def step(item, carry):
        a = (item >= whole[0]).astype(jnp.int32)
        some_runs(a, (item - a * whole[0]) * TILE, TILE)
        return carry

    lax.fori_loop(0, whole[0] + whole[1], step, 0)

    def remainder(a, carry):
        count = jnp.where(a == 0, counts[0], counts[1])
        start = count // TILE * TILE
        runs = TILE // 2
        while runs >= (1 if last else KEEP):

            @pl.when(count & runs != 0)
            def _():
                some_runs(a, start, runs)

            start = start + (count & runs)
            runs //= 2
        return carry

    lax.fori_loop(0, 2, remainder, 0)

    if not last:
        row = lax.broadcasted_iota(jnp.int32, meta.shape, 0)
        for a in range(2):
            start = counts[a] // KEEP * KEEP
            rest = counts[a] - start

            @pl.when((start > 0) & (rest > 0))
            def _():
                for n in range(KEEP - 1):
                    vbuf[a, n] = vbuf[a, start + n]
                for n in range(KEEP // 2):
                    kbuf[a, n] = kbuf[a, start // 2 + n]

            meta = jnp.where(row == 2 + a, rest.astype(jnp.float32), meta)
        meta_ref[...] = meta
        return

    for a in range(2):
        for h in range(0, heads_kv, 2):
            done = []
            for g in (h, h + 1):
                total = jnp.sum(state_refs[1][a, g], axis=1, keepdims=True)
                part = state_refs[2][a, g] * (1.0 / total)
                done.append(part.reshape(RUN, group, -1))
            out_ref[a * RUN : (a + 1) * RUN, h * group : (h + 2) * group, :] = (
                jnp.concatenate(done, axis=1).astype(out_ref.dtype)
            )


class Attention:
    def __init__(self, q, group, half, room):
        self.q, self.group, self.half = q, group, half
        self.factor = math.log2(math.e) / math.sqrt(q.shape[3])
        heads_kv, rows, head_dim = q.shape[1:]
        self.block_rows = 2 * heads_kv * RUN + heads_kv * head_dim + 16
        slots = 2 * room + KEEP
        self.carried = [jax.ShapeDtypeStruct((8, 128), jnp.float32)]
        self.carried += [
            jax.ShapeDtypeStruct((2, heads_kv, rows, n), jnp.float32)
            for n in (128, 128, head_dim)
        ]
        self.carried += [
            jax.ShapeDtypeStruct((2, slots // 2, heads_kv * head_dim, 2 * RUN), q.dtype),
            jax.ShapeDtypeStruct((2, slots, heads_kv * RUN, head_dim), q.dtype),
        ]

    def call(self, kernel, operands, shapes, aliases, count, name):
        vmem = pl.BlockSpec(memory_space=pltpu.VMEM)
        return pl.pallas_call(
            kernel,
            out_shape=shapes,
            in_specs=[vmem] * len(operands),
            out_specs=[vmem] * len(shapes),
            input_output_aliases=aliases,
            compiler_params=pltpu.CompilerParams(vmem_limit_bytes=28 * 1024 * 1024),
            cost_estimate=pl.CostEstimate(
                flops=count * RUN * self.q.size * 4,
                bytes_accessed=self.q.size * 8,
                transcendentals=0,
            ),
            name=name,
        )(*operands)

    def start(self, own):
        kernel = functools.partial(own_kernel, self.group, self.factor, self.half)
        return self.call(kernel, [self.q, own], self.carried, {}, 2, "attend_own")

    def add(self, state, kvs, out=None):
        kvs = [x if isinstance(x, tuple) else (x, 0) for x in kvs]
        blocks = [(skip, x.shape[0] // self.block_rows) for x, skip in kvs]
        count = sum(end - skip for skip, end in blocks)
        operands = [self.q, *(x for x, _ in kvs), *state]
        first, ahead = 1 + len(kvs), int(out is not None)
        aliases = {first + n: ahead + n for n in range(len(state))}
        shapes = ([out] if ahead else []) + self.carried
        kernel = functools.partial(
            attend_kernel, self.group, self.factor, self.half, out is not None, blocks
        )
        results = self.call(kernel, operands, shapes, aliases, count, "attend")
        return results[0] if ahead else results


def per_device(queries, keys, values, positions):
    outer, inner = lax.axis_size("outer"), lax.axis_size("inner")
    tokens, heads_q, head_dim = queries.shape
    heads_kv = keys.shape[1]
    group = heads_q // heads_kv
    half = tokens // RUN * outer * inner // 2

    chips = outer // 2
    bits = inner.bit_length() - 1
    ring = [0] + list(range(1, chips, 2)) + list(range(2, chips, 2))[::-1]
    after = {ring[n]: ring[(n + 1) % chips] for n in range(chips)}

    def permute(x, to):
        pairs = []
        for z in range(chips):
            for core in range(2):
                for place in range(inner):
                    nz, ncore, nplace = to(z, core, place)
                    pairs.append(
                        (
                            (2 * z + core) * inner + place,
                            (2 * nz + ncore) * inner + nplace,
                        )
                    )
        return lax.ppermute(x, AXES, pairs)

    def along_z(x):
        return permute(x, lambda z, core, place: (after[z], core, place))

    def over_place(x, step):
        def to(z, core, place):
            return z, core, place ^ (1 << (bits - 1 - step if core else step))

        return permute(x, to)

    def other_core(x):
        return permute(x, lambda z, core, place: (z, 1 - core, place))

    def tied(x, *others):
        return lax.optimization_barrier((x, *others))[0]

    by_run = values.reshape(2, RUN, heads_kv, head_dim).transpose(0, 2, 1, 3)
    numbers = (positions // RUN).astype(jnp.bfloat16)
    own = jnp.concatenate(
        [
            keys.reshape(tokens, -1).T,
            by_run.reshape(-1, head_dim),
            jnp.broadcast_to(numbers[None, :], (16, tokens)),
        ]
    )
    q = (
        queries.reshape(2, RUN, heads_kv, group, head_dim)
        .transpose(0, 2, 1, 3, 4)
        .reshape(2, heads_kv, RUN * group, head_dim)
    )
    block_rows = own.shape[0]

    attention = Attention(q, group, half, 2 * inner)
    state = attention.start(own)

    planes, ready = [], []
    stage = own
    for n in range(chips):
        following = along_z(stage) if n + 1 < chips else None
        if n < 2:
            held = stage
            for step in range(bits):
                if n == 0 and step == 1:
                    held = tied(held, following, state[0])
                there = over_place(held, step)
                held = jnp.concatenate([held, there])
            found = [
                held[m * block_rows : (m + 1) * block_rows] for m in range(inner)
            ]
        else:
            state = attention.add(state, ready[n - 2])
            found = [
                stage
                if m == 0
                else over_place(stage, m.bit_length() - 1)
                if m & (m - 1) == 0
                else along_z(tied(planes[-1][m], state[0]))
                for m in range(inner)
            ]
            held = jnp.concatenate(found)
        planes.append(found)
        stage = following
        if n + 1 < chips:
            ready.append([(held, int(n == 0)), other_core(held)])
    state = attention.add(state, ready[-1])
    held = tied(held, state[0])
    state = attention.add(state, [held])
    out = jax.ShapeDtypeStruct(queries.shape, queries.dtype)
    return attention.add(state, [other_core(held)], out)


def solution(mesh):
    in_specs = (
        P(("outer", "inner"), None, None),
        P(("outer", "inner"), None, None),
        P(("outer", "inner"), None, None),
        P(("outer", "inner")),
    )
    out_specs = P(("outer", "inner"), None, None)
    return jax.shard_map(
        per_device, mesh=mesh, in_specs=in_specs, out_specs=out_specs, check_vma=False
    )
```

time: 72.9 us -> 79 us (1.084)
  the two profiles are of different devices: /device:TPU:12 before, /device:TPU:0 now
where the time goes in v1:
time: 79 us; the launch traced here: 79.4 us
  waiting for transfers between devices  36.7 us (46%)
  Pallas kernels  25.1 us (32%)
  starting transfers between devices  13.9 us (18%)
  local copies, waits for them, and re-layouts  2.61 us (3%)
  other arithmetic  0.83 us (1%)
    ppermute x17, waiting for transfers between devices, permute(): return lax.ppermute(x, AXES, pairs)  36.7 us
    pallas_call x6, Pallas kernels, call(): pl.pallas_call(kernel, out_shape=shapes, in_specs=[vmem] * len(operands),...  25.1 us
    ppermute x17, starting transfers between devices, permute(): return lax.ppermute(x, AXES, pairs)  13.9 us
  transfers between devices with their start and end apart: 17, of which 8 were waited for; matrix products, arithmetic and copies ran while one was open for 1% of the time, Pallas kernels for 18%

profile of v1, /device:TPU:0, one launch (start us, length us, event | category | flops | bytes accessed | tf_op | source)
XLA Modules:
  0.0 79.4 jit_solution(15929664006422383864)
XLA Ops:
  0.0 1.1 %copy.36 = bf16[128,4,128]{0,2,1:T(8,128)(2,1)S(1)} copy(bf16[128,4,128]{2,1,0:T(4,128)(2,1)} %param.5) | data formatting | bytes 262144 | tf_op args[1]
  1.1 0.9 %copy.37 = bf16[2,64,4,128]{3,1,2,0:T(8,128)(2,1)S(1)} copy(bf16[2,64,4,128]{3,2,1,0:T(4,128)(2,1)} %bitcast.24) | data formatting | bytes 262144 | tf_op jit(solution)/shard_map/reshape | solution.py:316
  2.1 0.7 fusion
  2.8 3.0 %collective-permute-start.7 = (bf16[1040,128]{1,0:T(8,128)(2,1)S(1)}, bf16[1040,128]{1,0:T(8,128)(2,1)S(1)}, u32[]{:S(2)}, u32[]{:S(2)}) collective-permute-start(bf16[1040,128]{1,0:T(8,128)(2,1)S(1)} %pad_maximum_fusion.3.own_ref), channel_id=1, source_target_pairs={{0,1},{1,0},{2,3},{3,2},{4,6},{5,7},{6,4},{7,5},{8,9},{9,8},{10,11... | collective-permute-start | bytes 798728 | tf_op jit(solution)/shard_map/ppermute | solution.py:299
  5.8 1.6 %collective-permute-start = (bf16[1040,128]{1,0:T(8,128)(2,1)S(1)}, bf16[1040,128]{1,0:T(8,128)(2,1)S(1)}, u32[]{:S(2)}, u32[]{:S(2)}) collective-permute-start(bf16[1040,128]{1,0:T(8,128)(2,1)S(1)} %pad_maximum_fusion.3.own_ref), channel_id=1, source_target_pairs={{0,8},{1,9},{2,10},{3,11},{4,12},{5,13},{6,14},{7,15},{8,24},{9,25... | collective-permute-start | bytes 798728 | tf_op jit(solution)/shard_map/ppermute | solution.py:299
  7.3 0.0 copy-done
  7.3 0.2 copy.39
  7.5 1.2 %attend_own.1 = (f32[8,128]{1,0:T(8,128)S(1)}, f32[2,4,512,128]{3,2,1,0:T(8,128)S(1)}, f32[2,4,512,128]{3,2,1,0:T(8,128)S(1)}, f32[2,4,512,128]{3,2,1,0:T(8,128)...) custom-call(bf16[2,4,512,128]{3,2,1,0:T(8,128)(2,1)S(1)} %bitcast.13, ...), custom_call_target="tpu_custom_call" | custom-call | flops 268435456 | bytes 4194304 | tf_op jit(solution)/shard_map/attend_own/pallas_call | solution.py:241
  8.7 1.5 %collective-permute-done.7 = bf16[1040,128]{1,0:T(8,128)(2,1)S(1)} collective-permute-done((bf16[1040,128]{1,0:T(8,128)(2,1)S(1)}, bf16[1040,128]{1,0:T(8,128)(2,1)S(1)}, u32[]{:S(2)}, u32[]{:S(2)}) %collective-permute-start.7) | collective-permute-done | bytes 266272 | tf_op jit(solution)/shard_map/ppermute | solution.py:299
  10.2 4.3 %collective-permute-done = bf16[1040,128]{1,0:T(8,128)(2,1)S(1)} collective-permute-done((bf16[1040,128]{1,0:T(8,128)(2,1)S(1)}, bf16[1040,128]{1,0:T(8,128)(2,1)S(1)}, u32[]{:S(2)}, u32[]{:S(2)}) %collective-permute-start) | collective-permute-done | bytes 266272 | tf_op jit(solution)/shard_map/ppermute | solution.py:299
  14.5 0.5 collective-permute-start.8
  15.0 1.5 %collective-permute-start.5 = (bf16[1040,128]{1,0:T(8,128)(2,1)S(1)}, bf16[1040,128]{1,0:T(8,128)(2,1)S(1)}, u32[]{:S(2)}, u32[]{:S(2)}) collective-permute-start(bf16[1040,128]{1,0:T(8,128)(2,1)S(1)} %collective-permute-done), channel_id=1, source_target_pairs={{0,1},{1,0},{2,3},{3,2},{4,6},{5,7},{6,4},{7,5},{8,9},{9,8},{10,11... | collective-permute-start | bytes 798728 | tf_op jit(solution)/shard_map/ppermute | solution.py:299
  16.6 0.8 %collective-permute-start.1 = (bf16[1040,128]{1,0:T(8,128)(2,1)S(1)}, bf16[1040,128]{1,0:T(8,128)(2,1)S(1)}, u32[]{:S(2)}, u32[]{:S(2)}) collective-permute-start(bf16[1040,128]{1,0:T(8,128)(2,1)S(1)} %collective-permute-done), channel_id=1, source_target_pairs={{0,8},{1,9},{2,10},{3,11},{4,12},{5,13},{6,14},{7,15},{8,24},{9,25... | collective-permute-start | bytes 798728 | tf_op jit(solution)/shard_map/ppermute | solution.py:299
  17.4 6.9 %collective-permute-done.5 = bf16[1040,128]{1,0:T(8,128)(2,1)S(1)} collective-permute-done((bf16[1040,128]{1,0:T(8,128)(2,1)S(1)}, bf16[1040,128]{1,0:T(8,128)(2,1)S(1)}, u32[]{:S(2)}, u32[]{:S(2)}) %collective-permute-start.5) | collective-permute-done | bytes 266272 | tf_op jit(solution)/shard_map/ppermute | solution.py:299
  24.4 0.3 collective-permute-start.6
  24.7 2.0 %collective-permute-done.8 = bf16[2080,128]{1,0:T(8,128)(2,1)S(1)} collective-permute-done((bf16[2080,128]{1,0:T(8,128)(2,1)S(1)}, bf16[2080,128]{1,0:T(8,128)(2,1)S(1)}, u32[]{:S(2)}, u32[]{:S(2)}) %collective-permute-start.8) | collective-permute-done | bytes 532512 | tf_op jit(solution)/shard_map/ppermute | solution.py:299
  26.7 0.1 constant_dynamic-update-slice_fusion.refs_0_
  26.7 0.1 collective-permute-start.9
  26.8 0.0 collective-permute-done.1
  26.9 0.7 collective-permute-start.13
  27.6 0.7 collective-permute-start.14
  28.3 0.8 collective-permute-start.2
  29.1 7.5 %collective-permute-done.6 = bf16[2080,128]{1,0:T(8,128)(2,1)S(1)} collective-permute-done((bf16[2080,128]{1,0:T(8,128)(2,1)S(1)}, bf16[2080,128]{1,0:T(8,128)(2,1)S(1)}, u32[]{:S(2)}, u32[]{:S(2)}) %collective-permute-start.6) | collective-permute-done | bytes 532512 | tf_op jit(solution)/shard_map/ppermute | solution.py:299
  36.6 0.1 constant_dynamic-update-slice_fusion.2.refs_0_
  36.6 0.1 collective-permute-start.11
  36.8 0.0 collective-permute-done.9.refs_1_
  36.8 4.7 %attend.5 = (f32[8,128]{1,0:T(8,128)S(1)}, f32[2,4,512,128]{3,2,1,0:T(8,128)S(1)}, f32[2,4,512,128]{3,2,1,0:T(8,128)S(1)}, f32[2,4,512,128]{3,2,1,0:T(8,128)S(1)...) custom-call(bf16[2,4,512,128]{3,2,1,0:T(8,128)(2,1)S(1)} %bitcast.14, ...), custom_call_target="tpu_custom_call", output_to_operand_aliasing={{0}: (3, {}), {1}: (4, {}), {2}: (5, {}), {3}: (6, {}), {4}... | custom-call | flops 939524096 | bytes 4194304 | tf_op jit(solution)/shard_map/attend/pallas_call | solution.py:241
  41.5 0.1 collective-permute-start.10
  41.5 0.0 collective-permute-done.13
  41.6 0.0 collective-permute-done.14
  41.6 7.2 %collective-permute-done.10 = bf16[1040,128]{1,0:T(8,128)(2,1)S(1)} collective-permute-done((bf16[1040,128]{1,0:T(8,128)(2,1)S(1)}, bf16[1040,128]{1,0:T(8,128)(2,1)S(1)}, u32[]{:S(2)}, u32[]{:S(2)}) %collective-permute-start.10) | collective-permute-done | bytes 266272 | tf_op jit(solution)/shard_map/ppermute | solution.py:299
  48.9 0.1 collective-permute-start.15
  48.9 0.0 collective-permute-done.2
  48.9 0.8 %collective-permute-start.3 = (bf16[1040,128]{1,0:T(8,128)(2,1)S(1)}, bf16[1040,128]{1,0:T(8,128)(2,1)S(1)}, u32[]{:S(2)}, u32[]{:S(2)}) collective-permute-start(bf16[1040,128]{1,0:T(8,128)(2,1)S(1)} %collective-permute-done.2), channel_id=1, source_target_pairs={{0,1},{1,0},{2,3},{3,2},{4,6},{5,7},{6,4},{7,5},{8,9},{9,8},{10,11... | collective-permute-start | bytes 798728 | tf_op jit(solution)/shard_map/ppermute | solution.py:299
  49.8 2.7 %collective-permute-start.4 = (bf16[1040,128]{1,0:T(8,128)(2,1)S(1)}, bf16[1040,128]{1,0:T(8,128)(2,1)S(1)}, u32[]{:S(2)}, u32[]{:S(2)}) collective-permute-start(bf16[1040,128]{1,0:T(8,128)(2,1)S(1)} %collective-permute-done.2), channel_id=1, source_target_pairs={{0,2},{1,3},{2,0},{3,1},{4,5},{5,4},{6,7},{7,6},{8,10},{9,11},{10,... | collective-permute-start | bytes 798728 | tf_op jit(solution)/shard_map/ppermute | solution.py:299
  52.5 0.0 collective-permute-done.11.refs_1_
  52.5 4.8 %attend.6 = (f32[8,128]{1,0:T(8,128)S(1)}, f32[2,4,512,128]{3,2,1,0:T(8,128)S(1)}, f32[2,4,512,128]{3,2,1,0:T(8,128)S(1)}, f32[2,4,512,128]{3,2,1,0:T(8,128)S(1)...) custom-call(bf16[2,4,512,128]{3,2,1,0:T(8,128)(2,1)S(1)} %bitcast.15, ...), custom_call_target="tpu_custom_call", output_to_operand_aliasing={{0}: (3, {}), {1}: (4, {}), {2}: (5, {}), {3}: (6, {}), {4}... | custom-call | flops 1073741824 | bytes 4194304 | tf_op jit(solution)/shard_map/attend/pallas_call | solution.py:241
  57.4 0.1 collective-permute-start.12
  57.4 0.0 collective-permute-done.3
  57.4 0.3 collective-permute-done.4
  57.7 7.0 %collective-permute-done.12 = bf16[1040,128]{1,0:T(8,128)(2,1)S(1)} collective-permute-done((bf16[1040,128]{1,0:T(8,128)(2,1)S(1)}, bf16[1040,128]{1,0:T(8,128)(2,1)S(1)}, u32[]{:S(2)}, u32[]{:S(2)}) %collective-permute-start.12) | collective-permute-done | bytes 266272 | tf_op jit(solution)/shard_map/ppermute | solution.py:299
  64.7 0.1 pad_maximum_fusion.refs_0_
  64.8 0.0 collective-permute-done.15.refs_1_
  64.8 5.1 %attend.7 = (f32[8,128]{1,0:T(8,128)S(1)}, f32[2,4,512,128]{3,2,1,0:T(8,128)S(1)}, f32[2,4,512,128]{3,2,1,0:T(8,128)S(1)}, f32[2,4,512,128]{3,2,1,0:T(8,128)S(1)...) custom-call(bf16[2,4,512,128]{3,2,1,0:T(8,128)(2,1)S(1)} %bitcast.16, ...), custom_call_target="tpu_custom_call", output_to_operand_aliasing={{0}: (3, {}), {1}: (4, {}), {2}: (5, {}), {3}: (6, {}), {4}... | custom-call | flops 1073741824 | bytes 4194304 | tf_op jit(solution)/shard_map/attend/pallas_call | solution.py:241
  69.9 0.1 collective-permute-start.16
  70.0 3.3 %attend.8 = (f32[8,128]{1,0:T(8,128)S(1)}, f32[2,4,512,128]{3,2,1,0:T(8,128)S(1)}, f32[2,4,512,128]{3,2,1,0:T(8,128)S(1)}, f32[2,4,512,128]{3,2,1,0:T(8,128)S(1)...) custom-call(bf16[2,4,512,128]{3,2,1,0:T(8,128)(2,1)S(1)} %bitcast.17, ...), custom_call_target="tpu_custom_call", output_to_operand_aliasing={{0}: (2, {}), {1}: (3, {}), {2}: (4, {}), {3}: (5, {}), {4}... | custom-call | flops 536870912 | bytes 4194304 | tf_op jit(solution)/shard_map/attend/pallas_call | solution.py:241
  73.3 0.0 collective-permute-done.16.refs_0_
  73.3 6.1 %attend.9 = (bf16[128,32,128]{2,1,0:T(8,128)(2,1)}, f32[8,128]{1,0:T(8,128)S(1)}, f32[2,4,512,128]{3,2,1,0:T(8,128)S(1)}, f32[2,4,512,128]{3,2,1,0:T(8,128)S(1)}...) custom-call(bf16[2,4,512,128]{3,2,1,0:T(8,128)(2,1)S(1)} %bitcast.18, ...), custom_call_target="tpu_custom_call", output_to_operand_aliasing={{1}: (2, {}), {2}: (3, {}), {3}: (4, {}), {4}: (5, {}), {5}... | custom-call | flops 536870912 | bytes 4194304 | tf_op jit(solution)/shard_map/attend/pallas_call | solution.py:241
  (13 shorter events, 0.3 us)
Async XLA Ops:
  0.0 7.3 %copy-start = (bf16[128,32,128]{2,1,0:T(8,128)(2,1)S(1)}, bf16[128,32,128]{2,1,0:T(8,128)(2,1)}, u32[]{:S(2)}) copy-start(bf16[128,32,128]{2,1,0:T(8,128)(2,1)} %param.4) | copy-start | bytes 3145732
  2.8 7.4 %collective-permute-start.7 = (bf16[1040,128]{1,0:T(8,128)(2,1)S(1)}, bf16[1040,128]{1,0:T(8,128)(2,1)S(1)}, u32[]{:S(2)}, u32[]{:S(2)}) collective-permute-start(bf16[1040,128]{1,0:T(8,128)(2,1)S(1)} %pad_maximum_fusion.3.own_ref), channel_id=1, source_target_pairs={{0,1},{1,0},{2,3},{3,2},{4,6},{5,7},{6,4},{7,5},{8,9},{9,8},{10,11... | collective-permute-start | bytes 798728 | tf_op jit(solution)/shard_map/ppermute | solution.py:299
  5.8 8.8 %collective-permute-start = (bf16[1040,128]{1,0:T(8,128)(2,1)S(1)}, bf16[1040,128]{1,0:T(8,128)(2,1)S(1)}, u32[]{:S(2)}, u32[]{:S(2)}) collective-permute-start(bf16[1040,128]{1,0:T(8,128)(2,1)S(1)} %pad_maximum_fusion.3.own_ref), channel_id=1, source_target_pairs={{0,8},{1,9},{2,10},{3,11},{4,12},{5,13},{6,14},{7,15},{8,24},{9,25... | collective-permute-start | bytes 798728 | tf_op jit(solution)/shard_map/ppermute | solution.py:299
  14.5 12.1 %collective-permute-start.8 = (bf16[2080,128]{1,0:T(8,128)(2,1)S(1)}, bf16[2080,128]{1,0:T(8,128)(2,1)S(1)}, u32[]{:S(2)}, u32[]{:S(2)}) collective-permute-start(bf16[2080,128]{1,0:T(8,128)(2,1)S(1)} %pad_maximum_fusion.2), channel_id=1, source_target_pairs={{0,2},{1,3},{2,0},{3,1},{4,5},{5,4},{6,7},{7,6},{8,10},{9,11},{10,... | collective-permute-start | bytes 1597448 | tf_op jit(solution)/shard_map/ppermute | solution.py:299
  15.0 9.3 %collective-permute-start.5 = (bf16[1040,128]{1,0:T(8,128)(2,1)S(1)}, bf16[1040,128]{1,0:T(8,128)(2,1)S(1)}, u32[]{:S(2)}, u32[]{:S(2)}) collective-permute-start(bf16[1040,128]{1,0:T(8,128)(2,1)S(1)} %collective-permute-done), channel_id=1, source_target_pairs={{0,1},{1,0},{2,3},{3,2},{4,6},{5,7},{6,4},{7,5},{8,9},{9,8},{10,11... | collective-permute-start | bytes 798728 | tf_op jit(solution)/shard_map/ppermute | solution.py:299
  16.6 10.3 %collective-permute-start.1 = (bf16[1040,128]{1,0:T(8,128)(2,1)S(1)}, bf16[1040,128]{1,0:T(8,128)(2,1)S(1)}, u32[]{:S(2)}, u32[]{:S(2)}) collective-permute-start(bf16[1040,128]{1,0:T(8,128)(2,1)S(1)} %collective-permute-done), channel_id=1, source_target_pairs={{0,8},{1,9},{2,10},{3,11},{4,12},{5,13},{6,14},{7,15},{8,24},{9,25... | collective-permute-start | bytes 798728 | tf_op jit(solution)/shard_map/ppermute | solution.py:299
  24.4 12.2 %collective-permute-start.6 = (bf16[2080,128]{1,0:T(8,128)(2,1)S(1)}, bf16[2080,128]{1,0:T(8,128)(2,1)S(1)}, u32[]{:S(2)}, u32[]{:S(2)}) collective-permute-start(bf16[2080,128]{1,0:T(8,128)(2,1)S(1)} %pad_maximum_fusion.1), channel_id=1, source_target_pairs={{0,2},{1,3},{2,0},{3,1},{4,5},{5,4},{6,7},{7,6},{8,10},{9,11},{10,... | collective-permute-start | bytes 1597448 | tf_op jit(solution)/shard_map/ppermute | solution.py:299
  26.7 10.0 %collective-permute-start.9 = (bf16[4160,128]{1,0:T(8,128)(2,1)S(1)}, bf16[4160,128]{1,0:T(8,128)(2,1)S(1)}, u32[]{:S(2)}, u32[]{:S(2)}) collective-permute-start(bf16[4160,128]{1,0:T(8,128)(2,1)S(1)} %constant_dynamic-update-slice_fusion.refs_0_), channel_id=1, source_target_pairs={{0,4},{1,5},{2,6},{3,7},{4,0},{5,1},{6,2},{7,3},{8,12},{9,13},{10,... | collective-permute-start | bytes 3194888 | tf_op jit(solution)/shard_map/ppermute | solution.py:299
  26.9 14.7 %collective-permute-start.13 = (bf16[1040,128]{1,0:T(8,128)(2,1)S(1)}, bf16[1040,128]{1,0:T(8,128)(2,1)S(1)}, u32[]{:S(2)}, u32[]{:S(2)}) collective-permute-start(bf16[1040,128]{1,0:T(8,128)(2,1)S(1)} %collective-permute-done.1), channel_id=1, source_target_pairs={{0,1},{1,0},{2,3},{3,2},{4,6},{5,7},{6,4},{7,5},{8,9},{9,8},{10,11... | collective-permute-start | bytes 798728 | tf_op jit(solution)/shard_map/ppermute | solution.py:299
  27.6 14.0 %collective-permute-start.14 = (bf16[1040,128]{1,0:T(8,128)(2,1)S(1)}, bf16[1040,128]{1,0:T(8,128)(2,1)S(1)}, u32[]{:S(2)}, u32[]{:S(2)}) collective-permute-start(bf16[1040,128]{1,0:T(8,128)(2,1)S(1)} %collective-permute-done.1), channel_id=1, source_target_pairs={{0,2},{1,3},{2,0},{3,1},{4,5},{5,4},{6,7},{7,6},{8,10},{9,11},{10,... | collective-permute-start | bytes 798728 | tf_op jit(solution)/shard_map/ppermute | solution.py:299
  28.3 20.7 %collective-permute-start.2 = (bf16[1040,128]{1,0:T(8,128)(2,1)S(1)}, bf16[1040,128]{1,0:T(8,128)(2,1)S(1)}, u32[]{:S(2)}, u32[]{:S(2)}) collective-permute-start(bf16[1040,128]{1,0:T(8,128)(2,1)S(1)} %collective-permute-done.1), channel_id=1, source_target_pairs={{0,8},{1,9},{2,10},{3,11},{4,12},{5,13},{6,14},{7,15},{8,24},{9,25... | collective-permute-start | bytes 798728 | tf_op jit(solution)/shard_map/ppermute | solution.py:299
  36.6 15.9 %collective-permute-start.11 = (bf16[4160,128]{1,0:T(8,128)(2,1)S(1)}, bf16[4160,128]{1,0:T(8,128)(2,1)S(1)}, u32[]{:S(2)}, u32[]{:S(2)}) collective-permute-start(bf16[4160,128]{1,0:T(8,128)(2,1)S(1)} %constant_dynamic-update-slice_fusion.2.refs_0_), channel_id=1, source_target_pairs={{0,4},{1,5},{2,6},{3,7},{4,0},{5,1},{6,2},{7,3},{8,12},{9,13},{10,... | collective-permute-start | bytes 3194888 | tf_op jit(solution)/shard_map/ppermute | solution.py:299
  41.5 7.4 %collective-permute-start.10 = (bf16[1040,128]{1,0:T(8,128)(2,1)S(1)}, bf16[1040,128]{1,0:T(8,128)(2,1)S(1)}, u32[]{:S(2)}, u32[]{:S(2)}) collective-permute-start(bf16[1040,128]{1,0:T(8,128)(2,1)S(1)} %slice.4), channel_id=1, source_target_pairs={{0,8},{1,9},{2,10},{3,11},{4,12},{5,13},{6,14},{7,15},{8,24},{9,25... | collective-permute-start | bytes 798728 | tf_op jit(solution)/shard_map/ppermute | solution.py:299
  48.9 15.9 %collective-permute-start.15 = (bf16[4160,128]{1,0:T(8,128)(2,1)S(1)}, bf16[4160,128]{1,0:T(8,128)(2,1)S(1)}, u32[]{:S(2)}, u32[]{:S(2)}) collective-permute-start(bf16[4160,128]{1,0:T(8,128)(2,1)S(1)} %constant_dynamic-update-slice_fusion.5.refs_0_), channel_id=1, source_target_pairs={{0,4},{1,5},{2,6},{3,7},{4,0},{5,1},{6,2},{7,3},{8,12},{9,13},{10,... | collective-permute-start | bytes 3194888 | tf_op jit(solution)/shard_map/ppermute | solution.py:299
  48.9 8.5 %collective-permute-start.3 = (bf16[1040,128]{1,0:T(8,128)(2,1)S(1)}, bf16[1040,128]{1,0:T(8,128)(2,1)S(1)}, u32[]{:S(2)}, u32[]{:S(2)}) collective-permute-start(bf16[1040,128]{1,0:T(8,128)(2,1)S(1)} %collective-permute-done.2), channel_id=1, source_target_pairs={{0,1},{1,0},{2,3},{3,2},{4,6},{5,7},{6,4},{7,5},{8,9},{9,8},{10,11... | collective-permute-start | bytes 798728 | tf_op jit(solution)/shard_map/ppermute | solution.py:299
  49.8 7.9 %collective-permute-start.4 = (bf16[1040,128]{1,0:T(8,128)(2,1)S(1)}, bf16[1040,128]{1,0:T(8,128)(2,1)S(1)}, u32[]{:S(2)}, u32[]{:S(2)}) collective-permute-start(bf16[1040,128]{1,0:T(8,128)(2,1)S(1)} %collective-permute-done.2), channel_id=1, source_target_pairs={{0,2},{1,3},{2,0},{3,1},{4,5},{5,4},{6,7},{7,6},{8,10},{9,11},{10,... | collective-permute-start | bytes 798728 | tf_op jit(solution)/shard_map/ppermute | solution.py:299
  57.4 7.4 %collective-permute-start.12 = (bf16[1040,128]{1,0:T(8,128)(2,1)S(1)}, bf16[1040,128]{1,0:T(8,128)(2,1)S(1)}, u32[]{:S(2)}, u32[]{:S(2)}) collective-permute-start(bf16[1040,128]{1,0:T(8,128)(2,1)S(1)} %collective-permute-done.10), channel_id=1, source_target_pairs={{0,8},{1,9},{2,10},{3,11},{4,12},{5,13},{6,14},{7,15},{8,24},{9,25... | collective-permute-start | bytes 798728 | tf_op jit(solution)/shard_map/ppermute | solution.py:299
  69.9 3.4 %collective-permute-start.16 = (bf16[4160,128]{1,0:T(8,128)(2,1)S(1)}, bf16[4160,128]{1,0:T(8,128)(2,1)S(1)}, u32[]{:S(2)}, u32[]{:S(2)}) collective-permute-start(bf16[4160,128]{1,0:T(8,128)(2,1)S(1)} %pad_maximum_fusion.refs_0_), channel_id=1, source_target_pairs={{0,4},{1,5},{2,6},{3,7},{4,0},{5,1},{6,2},{7,3},{8,12},{9,13},{10,... | collective-permute-start | bytes 3194888 | tf_op jit(solution)/shard_map/ppermute | solution.py:299
